TPU v7x, 32 devices: a whole 2x2x4 slice. The times are simulated.
32 devices in a mesh: band: 4 (over x, core), row: 4 (over z), col: 2 (over y).
Axes of the slice: x: 2, y: 2, z: 4, core: 2. Of those that a mesh axis runs over, the one named last changes fastest.
Arguments:
- tokens: bfloat16 [256, 4, 16, 1024], P(('band', 'row'), 'col'), may hold values from -10 to 10
- counts: int32 [4], replicated, may hold values from 1 to 4, as said below
- norm_band: bfloat16 [1024], replicated, may hold values from 0.099609375 to 1.8984375
- w_band_qkv: bfloat16 [1024, 1536], replicated, may hold values from -1 to 1
- w_band_out: bfloat16 [512, 1024], replicated, may hold values from -0.25 to 0.25
- norm_space: bfloat16 [1024], replicated, may hold values from 0.099609375 to 1.8984375
- w_space_qkv: bfloat16 [1024, 1536], replicated, may hold values from -1 to 1
- w_space_out: bfloat16 [512, 1024], replicated, may hold values from -0.25 to 0.25
Outputs:
- layer_out: bfloat16 [256, 4, 16, 1024], P(('band', 'row'), 'col')
Inputs may be any that keep to these rules, and one draw needn't show every extreme that they name: `counts`: every group holds at least one live token; some group is full and some group holds exactly one.
All inputs are finite; a program needn't handle non-finite values.
Results may differ from a plain program's by a relative error of at most 0.0063.
Values may be sent and summed in bfloat16 or wider, within the bound.
A program may use at most 128 MiB of HBM per device.

v0:
```python
import jax
import jax.numpy as jnp
from jax import lax
from jax.sharding import PartitionSpec as P

HD = 64
HB = 8
HR = 4
HC = 4


EPS = 1e-06


def rms_norm(values, gain):
    wide = values.astype(jnp.float32)
    scale = lax.rsqrt(jnp.mean(wide * wide, axis=-1, keepdims=True) + EPS)
    return (wide * scale * gain.astype(jnp.float32)).astype(jnp.bfloat16)


def online_step(carry, scores, values, out_form):
    top, total, accum = carry
    new_top = jnp.maximum(top, jnp.max(scores, axis=-1))
    probs = jnp.exp(scores - new_top[..., None])
    total = jnp.sum(probs, axis=-1)
    accum = jnp.einsum(
        out_form, probs.astype(jnp.bfloat16), values, preferred_element_type=jnp.float32
    )
    return (new_top, total, accum)


def start_carry(shape):
    return (
        jnp.full(shape, -1e30, jnp.float32),
        jnp.zeros(shape, jnp.float32),
        jnp.zeros(shape + (HD,), jnp.float32),
    )


def local(tokens, counts, norm_band, w_band_qkv, w_band_out, norm_space, w_space_qkv, w_space_out):
    prows, pcols, slots, width = tokens.shape
    patches = prows * pcols
    scale = HD ** (-0.5)
    groups = counts.shape[0]
    normed = rms_norm(tokens, norm_band)
    band_qkv = jnp.dot(
        normed.reshape(-1, width), w_band_qkv, preferred_element_type=jnp.float32
    ).astype(jnp.bfloat16)
    parts = band_qkv.reshape(patches, slots, 3, HB, HD)
    slot_ids = lax.iota(jnp.int32, slots)
    group_of = slot_ids // (slots // groups)
    lookup = jnp.sum(
        jnp.where(group_of[:, None] == lax.iota(jnp.int32, groups)[None, :], counts[None, :], 0),
        axis=-1,
    )
    live = slot_ids % (slots // groups) < lookup
    scores = (
        jnp.einsum(
            "pihd,pjhd->phij", parts[:, :, 0], parts[:, :, 1], preferred_element_type=jnp.float32
        )
        * scale
    )
    scores = jnp.where(live[None, None, None, :], scores, -1e30)
    top = jnp.max(scores, axis=-1, keepdims=True)
    probs = jnp.exp(scores - top)
    total = jnp.sum(probs, axis=-1)
    mixed = jnp.einsum(
        "phij,pjhd->pihd",
        probs.astype(jnp.bfloat16),
        parts[:, :, 2],
        preferred_element_type=jnp.float32,
    )
    mixed = mixed / jnp.transpose(total, (0, 2, 1))[..., None]
    band_heads = mixed.astype(jnp.bfloat16).reshape(patches * slots, HB * HD)
    resid = tokens.astype(jnp.float32) + jnp.dot(
        band_heads, w_band_out, preferred_element_type=jnp.float32
    ).reshape(prows, pcols, slots, width)
    normed2 = rms_norm(resid, norm_space)
    space_qkv = jnp.dot(
        normed2.reshape(-1, width), w_space_qkv, preferred_element_type=jnp.float32
    ).astype(jnp.bfloat16)
    space_qkv = space_qkv.reshape(prows, pcols, slots, 3, (HR + HC) * HD)
    row_part = space_qkv[..., : HR * HD]
    col_part = space_qkv[..., HR * HD :]
    block = lax.all_to_all(row_part, "col", split_axis=0, concat_axis=1, tiled=True)
    lines = block.shape[0]
    across = block.shape[1]
    many = block.shape[2]
    pieces = block.reshape(lines, across, many, 3, HR, HD)
    line_scores = (
        jnp.einsum(
            "rishd,rjshd->rshij",
            pieces[:, :, :, 0],
            pieces[:, :, :, 1],
            preferred_element_type=jnp.float32,
        )
        * scale
    )
    line_top = jnp.max(line_scores, axis=-1, keepdims=True)
    line_probs = jnp.exp(line_scores - line_top)
    line_total = jnp.sum(line_probs, axis=-1)
    line_mixed = jnp.einsum(
        "rshij,rjshd->rishd",
        line_probs.astype(jnp.bfloat16),
        pieces[:, :, :, 2],
        preferred_element_type=jnp.float32,
    )
    line_mixed = line_mixed / jnp.transpose(line_total, (0, 3, 1, 2))[..., None]
    line_mixed = line_mixed.astype(jnp.bfloat16).reshape(lines, across, many, HR * HD)
    row_heads = lax.all_to_all(line_mixed, "col", split_axis=1, concat_axis=0, tiled=True)
    col_query = col_part[:, :, :, 0].reshape(prows, pcols, slots, HC, HD)
    piece = lax.all_gather(col_part[:, :, :, 1:], ("band", "row"), axis=0, tiled=True)
    many = piece.shape[0]
    keys = piece[:, :, :, 0].reshape(many, pcols, slots, HC, HD)
    vals = piece[:, :, :, 1].reshape(many, pcols, slots, HC, HD)
    col_scores = (
        jnp.einsum("icshd,jcshd->cshij", col_query, keys, preferred_element_type=jnp.float32)
        * scale
    )
    ctop, ctotal, caccum = online_step(
        start_carry((pcols, slots, HC, prows)), col_scores, vals, "cshij,jcshd->cshid"
    )
    col_heads = (
        (caccum / ctotal[..., None])
        .transpose(3, 0, 1, 2, 4)
        .astype(jnp.bfloat16)
        .reshape(prows, pcols, slots, HC * HD)
    )
    heads = jnp.concatenate([row_heads, col_heads], axis=-1)
    projected = jnp.dot(
        heads.reshape(-1, (HR + HC) * HD), w_space_out, preferred_element_type=jnp.float32
    )
    return (resid + projected.reshape(prows, pcols, slots, width)).astype(jnp.bfloat16)


def solution(mesh):
    placed = (P(("band", "row"), "col", None, None), P(), P(), P(), P(), P(), P(), P())
    return jax.shard_map(
        local,
        mesh=mesh,
        in_specs=placed,
        out_specs=P(("band", "row"), "col", None, None),
        check_vma=False,
    )
```

profile of v0, /device:TPU:0, one launch (start us, length us, event | category | flops | bytes accessed | tf_op | source)
XLA Modules:
  0.0 158.2 jit_solution(14184369864026664447)
XLA Ops:
  6.5 0.9 select_reduce_fusion
  7.4 0.7 convert_element_type.44
  8.2 0.7 convert_element_type.49
  8.9 1.5 fusion
  10.4 1.5 fusion.2
  11.9 2.9 %convolution_convert_fusion.1 = bf16[512,1536]{1,0:T(8,128)(2,1)} fusion(bf16[512,1024]{1,0:T(8,128)(2,1)S(1)} %bitcast.91, bf16[1024,1536]{1,0:T(8,128)(2,1)S(1)} %copy-done), kind=kOutput, calls=%fused_computation.4 | convolution fusion | flops 1611399168 | bytes 5767168 | tf_op jit(solution)/shard_map/dot_general | solution.py:46
  14.9 4.0 %reshape.88 = bf16[32,16,3,8,64]{4,3,2,1,0:T(8,128)(2,1)S(1)} reshape(bf16[512,1536]{1,0:T(8,128)(2,1)} %convolution_convert_fusion.1) | data formatting | bytes 3145728 | tf_op jit(solution)/shard_map/reshape | solution.py:49
  18.9 0.9 fusion.39
  19.8 0.8 fusion.4
  20.6 0.9 fusion.7
  21.5 1.4 fusion.3
  22.9 0.0 copy-start.3
  22.9 0.3 copy.56
  23.2 1.4 dot_general.37
  24.6 2.2 %multiply_reduce_fusion = (f32[16,2,16]{2,1,0:T(2,128)S(1)}, f32[16,2,16,1024]{3,2,1,0:T(8,128)S(1)}) fusion(bf16[16,2,16,512]{3,2,1,0:T(8,128)(2,1)} %dot_general.37, bf16[512,1024]{1,0:T(8,128)(2,1)} %param.12, bf16[16,2,16,1024]{3,2,1,0:T(8,128)(2,1)S(1)} %copy-done.3), kind=kOutput, calls=%fused_computation.13 | convolution fusion | flops 538967552 | bytes 4720640 | tf_op jit(solution)/shard_map/dot_general | solution.py:75
  26.8 0.2 multiply_convert_fusion
  27.1 2.4 %copy-done.5 = bf16[1024,1536]{1,0:T(8,128)(2,1)S(1)} copy-done((bf16[1024,1536]{1,0:T(8,128)(2,1)S(1)}, bf16[1024,1536]{1,0:T(8,128)(2,1)}, u32[]{:S(2)}) %copy-start.5) | copy-done | bytes 3145752
  29.4 2.9 %convolution_convert_fusion = bf16[512,1536]{1,0:T(8,128)(2,1)} fusion(bf16[512,1024]{1,0:T(8,128)(2,1)S(1)} %bitcast.92, bf16[1024,1536]{1,0:T(8,128)(2,1)S(1)} %copy-done.5), kind=kOutput, calls=%fused_computation.3 | convolution fusion | flops 1611399168 | bytes 5767168 | tf_op jit(solution)/shard_map/dot_general | solution.py:79
  32.4 5.6 %reshape.90 = bf16[16,2,16,3,512]{4,3,2,1,0:T(4,128)(2,1)} reshape(bf16[512,1536]{1,0:T(8,128)(2,1)} %convolution_convert_fusion) | data formatting | bytes 3145728 | tf_op jit(solution)/shard_map/reshape | solution.py:82
  38.0 1.9 %slice.55 = bf16[16,2,16,2,256]{4,3,2,1,0:T(2,128)(2,1)S(1)} slice(bf16[16,2,16,3,512]{4,3,2,1,0:T(4,128)(2,1)} %reshape.90), slice={[0:16], [0:2], [0:16], [1:3], [256:512]} | slice | bytes 1048576 | tf_op jit(solution)/shard_map/slice | solution.py:112
  39.9 0.9 copy.67
  40.8 0.0 all-gather.2.cloned.1.call-update
  40.8 0.5 slice-done
  41.3 0.2 copy.57
  41.4 14.9 %all_to_all.30 = bf16[16,2,16,3,256]{4,2,3,1,0:T(8,128)(2,1)S(1)} all-to-all(bf16[16,2,16,3,256]{4,2,3,1,0:T(8,128)(2,1)S(1)} %copy.57), channel_id=1, replica_groups=mesh['band'=4,'row'=4,'col'=2] {'col'}, dimensions={0} | all-to-all | bytes 1572864 | tf_op jit(solution)/shard_map/all_to_all | solution.py:85
  56.4 0.1 copy.110
  56.4 0.7 reshape.91
  57.1 0.9 fusion.40
  58.1 1.4 fusion.41
  59.5 1.0 fusion.24
  60.4 1.3 fusion.12
  61.7 0.3 copy.76
  62.0 1.1 reshape.95
  63.1 3.7 %all-to-all-start.1 = ((bf16[8,4,16,256]{3,2,0,1:T(8,128)(2,1)}), bf16[8,4,16,256]{3,2,0,1:T(8,128)(2,1)S(1)}, u32[]{:S(2)}, u32[]{:S(2)}) async-start(bf16[8,4,16,256]{3,2,0,1:T(8,128)(2,1)} %reshape.95), calls=%async_computation.1 | async-start | bytes 524288 | tf_op jit(solution)/shard_map/all_to_all | solution.py:110
  66.8 1.4 slice_reduce_fusion
  68.2 0.2 reshape_squeeze.9
  68.4 3.3 %all-to-all-done.1 = bf16[8,4,16,256]{3,2,0,1:T(8,128)(2,1)S(1)} async-done(((bf16[8,4,16,256]{3,2,0,1:T(8,128)(2,1)}), bf16[8,4,16,256]{3,2,0,1:T(8,128)(2,1)S(1)}, u32[]{:S(2)}, u32[]{:S(2)}) %all-to-all-start.1) | async-done | bytes 262176 | tf_op jit(solution)/shard_map/all_to_all | solution.py:110
  71.7 0.7 copy.66
  72.4 46.1 %all-gather.2.cloned.1.call-done = bf16[256,2,16,2,256]{4,2,3,1,0:T(8,128)(2,1)} async-done(((bf16[16,2,16,2,256]{4,2,3,1,0:T(8,128)(2,1)}), bf16[256,2,16,2,256]{4,2,3,1,0:T(8,128)(2,1)}) %all-gather.2.cloned.1.call-update) | async-done | bytes 8388624 | tf_op jit(solution)/shard_map/all_gather | solution.py:112
  118.5 6.0 %fusion.38 = (bf16[256,2,16,1,256]{4,2,3,1,0:T(8,128)(2,1)}, bf16[256,2,16,1,256]{4,2,3,1,0:T(8,128)(2,1)}) fusion(bf16[256,2,16,2,256]{4,2,3,1,0:T(8,128)(2,1)} %all-gather.2.cloned.1.call-done), kind=kLoop, calls=%fused_computation.70 | loop fusion | bytes 16777216 | tf_op jit(solution)/shard_map/slice | solution.py:114
  124.5 7.5 %copy.68 = bf16[256,2,16,1,256]{0,4,2,1,3:T(8,128)(2,1)} copy(bf16[256,2,16,1,256]{4,2,3,1,0:T(8,128)(2,1)} %get-tuple-element.5) | data formatting | bytes 8388608 | tf_op jit(solution)/shard_map/slice | solution.py:114
  132.0 3.1 %multiply_reduce_fusion.1 = (f32[2,16,4,16]{3,2,1,0:T(4,128)S(1)}, f32[2,16,4,16,256]{4,3,2,1,0:T(8,128)S(1)}) fusion(bf16[256,2,16,4,64]{0,4,3,2,1:T(8,128)(2,1)} %bitcast.86, bf16[16,2,16,4,64]{4,3,2,1,0:T(4,128)(2,1)S(1)} %reshape_squeeze.9), kind=kOutput, calls=%fused_computation.16 | convolution fusion | flops 68155392 | bytes 6561792 | tf_op jit(solution)/shard_map/icshd,jcshd->cshij/dot_general | solution.py:117
  135.2 7.5 %copy.70 = bf16[256,2,16,1,256]{0,4,2,1,3:T(8,128)(2,1)} copy(bf16[256,2,16,1,256]{4,2,3,1,0:T(8,128)(2,1)} %get-tuple-element.6) | data formatting | bytes 8388608 | tf_op jit(solution)/shard_map/slice | solution.py:115
  142.7 0.7 fusion.5
  143.4 3.5 %fusion.10 = bf16[16,2,16,4,64]{4,0,3,2,1:T(8,128)(2,1)S(1)} fusion(bf16[256,2,16,4,64]{0,4,3,2,1:T(8,128)(2,1)} %bitcast.87, f32[2,16,4,16,256]{4,3,2,1,0:T(8,128)S(1)} %get-tuple-element.18, f32[2,16,4,16]{3,2,1,0:T(4,128)S(1)} %broadcast_maximum_fusion, f32[16,2,16,4]{0,3,2,1:T(4,128)S(1)} %bitcast.96), kind=kOutput, calls=%fused_computation.26 | convolution fusion | flops 68943872 | bytes 6569984 | tf_op jit(solution)/shard_map/cshij,jcshd->cshid/dot_general | solution.py:26
  146.9 0.3 copy.71
  147.2 0.3 concatenate.10
  147.5 3.8 %add_convert_fusion = bf16[16,2,16,1024]{3,2,1,0:T(8,128)(2,1)} fusion(f32[16,2,16,1024]{3,2,1,0:T(8,128)} %copy-done.2, bf16[512,1024]{1,0:T(8,128)(2,1)} %param.15, bf16[16,2,16,256]{3,2,1,0:T(8,128)(2,1)S(1)} %concatenate.10, bf16[16,2,16,256]{3,2,1,0:T(8,128)(2,1)} %bitcast.90), kind=kOutput, calls=%fused_computation.10 | convolution fusion | flops 538968064 | bytes 4718592 | tf_op jit(solution)/shard_map/dot_general | solution.py:130
  (17 shorter events, 0.1 us)
Async XLA Ops:
  6.5 5.4 %copy-start = (bf16[1024,1536]{1,0:T(8,128)(2,1)S(1)}, bf16[1024,1536]{1,0:T(8,128)(2,1)}, u32[]{:S(2)}) copy-start(bf16[1024,1536]{1,0:T(8,128)(2,1)} %param.11) | copy-start | bytes 9437188
  6.5 112.0 %all-gather.2.cloned.1.call-start = ((), (), s32[]{:S(2)}) async-start(), calls=%async_computation.2 | async-start | bytes 8912896 | tf_op jit(solution)/shard_map/all_gather | solution.py:112
  22.9 1.7 %copy-start.3 = (bf16[16,2,16,1024]{3,2,1,0:T(8,128)(2,1)S(1)}, bf16[16,2,16,1024]{3,2,1,0:T(8,128)(2,1)}, u32[]{:S(2)}) copy-start(bf16[16,2,16,1024]{3,2,1,0:T(8,128)(2,1)} %param.8) | copy-start | bytes 3145732
  26.8 5.6 %copy-start.2 = (f32[16,2,16,1024]{3,2,1,0:T(8,128)}, f32[16,2,16,1024]{3,2,1,0:T(8,128)S(1)}, u32[]{:S(2)}) copy-start(f32[16,2,16,1024]{3,2,1,0:T(8,128)S(1)} %get-tuple-element.16) | copy-start | bytes 6291460
  26.8 2.6 %copy-start.5 = (bf16[1024,1536]{1,0:T(8,128)(2,1)S(1)}, bf16[1024,1536]{1,0:T(8,128)(2,1)}, u32[]{:S(2)}) copy-start(bf16[1024,1536]{1,0:T(8,128)(2,1)} %param.14) | copy-start | bytes 9437188
  39.9 1.4 slice-start
  61.7 5.0 %copy-start.4 = (bf16[16,2,16,3,512]{4,3,2,1,0:T(4,128)(2,1)S(1)}, bf16[16,2,16,3,512]{4,3,2,1,0:T(4,128)(2,1)}, u32[]{:S(2)}) copy-start(bf16[16,2,16,3,512]{4,3,2,1,0:T(4,128)(2,1)} %reshape.90) | copy-start | bytes 4718596
  63.1 8.6 %all-to-all-start.1 = ((bf16[8,4,16,256]{3,2,0,1:T(8,128)(2,1)}), bf16[8,4,16,256]{3,2,0,1:T(8,128)(2,1)S(1)}, u32[]{:S(2)}, u32[]{:S(2)}) async-start(bf16[8,4,16,256]{3,2,0,1:T(8,128)(2,1)} %reshape.95), calls=%async_computation.1 | async-start | bytes 524288 | tf_op jit(solution)/shard_map/all_to_all | solution.py:110
  147.5 3.8 %copy-start.1 = (bf16[1024,1536]{1,0:T(8,128)(2,1)S(1)}, bf16[1024,1536]{1,0:T(8,128)(2,1)}, u32[]{:S(2)}) copy-start(bf16[1024,1536]{1,0:T(8,128)(2,1)} %param.11) | copy-start | bytes 9437188
Sparse Core Ops, SparseCore 0:
  40.9 77.5 all-gather.1
where the time goes:
time: 159 us; the launch traced here: 158 us
  waiting for transfers between devices  49.4 us (31%)
  local copies, waits for them, and re-layouts  45 us (28%)
  matrix products  23.4 us (15%)
  blocking collectives  14.9 us (9%)
  between operations  13.7 us (9%)
  other arithmetic  8.25 us (5%)
  starting transfers between devices  3.67 us (2%)
    all_gather x1, waiting for transfers between devices, local(): lax.all_gather(col_part[:, :, :, 1:], ('band', 'row'), axis=0, tiled=True)  46.1 us
    all_to_all x1, blocking collectives, local(): lax.all_to_all(row_part, 'col', split_axis=0, concat_axis=1, tiled=True)  14.9 us
    slice x2, local copies, waits for them, and re-layouts, local(): keys = piece[:, :, :, 0].reshape(many, pcols, slots, HC, HD)  13.5 us
    slice x1, local copies, waits for them, and re-layouts, local(): vals = piece[:, :, :, 1].reshape(many, pcols, slots, HC, HD)  7.51 us
    reshape x1, local copies, waits for them, and re-layouts, local(): space_qkv = space_qkv.reshape(prows, pcols, slots, 3, (HR + HC) * HD)  5.61 us
    reshape x1, local copies, waits for them, and re-layouts, local(): parts = band_qkv.reshape(patches, slots, 3, HB, HD)  3.97 us
    dot_general x1, matrix products, local(): jnp.dot(heads.reshape(-1, (HR + HC) * HD), w_space_out, preferred_element...  3.82 us
    all_to_all x1, starting transfers between devices, local(): lax.all_to_all(line_mixed, 'col', split_axis=1, concat_axis=0, tiled=True)  3.67 us
  transfers between devices with their start and end apart: 2, of which 2 were waited for; matrix products, arithmetic and copies ran while one was open for 6% of the time, Pallas kernels for 0%

commit v1 on v0

v1 whole, which is shorter than its diff:
```python
import functools

import jax
import jax.numpy as jnp
from jax import lax
from jax.experimental import pallas as pl
from jax.experimental.pallas import tpu as pltpu
from jax.sharding import PartitionSpec as P

HD = 64
HB = 8
HR = 4
HC = 4


EPS = 1e-06
LOG2E = 1.4426950408889634
MESH = pl.DeviceIdType.MESH
PAIR = 2 * HD


def rms_norm(wide, gain):
    scale = lax.rsqrt(jnp.mean(wide * wide, axis=-1, keepdims=True) + EPS)
    return (wide * scale * gain).astype(jnp.bfloat16)


def dot(left, right):
    return jnp.dot(left, right, preferred_element_type=jnp.float32)


def lane_masks():
    first = lax.broadcasted_iota(jnp.int32, (1, PAIR), 1) < HD
    wide = jnp.where(first, 1.0, 0.0)
    return first, wide.astype(jnp.bfloat16), (1.0 - wide).astype(jnp.bfloat16)


def attend(q, k, v, bias):
    first, even, odd = lane_masks()
    m = k.shape[0]
    keys = jnp.concatenate([k * even, k * odd], axis=0)
    vals = jnp.concatenate([v * even, v * odd], axis=0)
    scores = lax.dot_general(
        q, keys, (((1,), (1,)), ((), ())), preferred_element_type=jnp.float32
    )
    probs, totals = [], []
    for h in range(2):
        part = scores[:, h * m : (h + 1) * m] * (HD ** (-0.5) * LOG2E)
        if bias is not None:
            part = part + bias
        part = jnp.exp2(part - jnp.max(part, axis=-1, keepdims=True))
        totals.append(jnp.sum(part, axis=-1, keepdims=True))
        probs.append(part.astype(jnp.bfloat16))
    mixed = dot(jnp.concatenate(probs, axis=1), vals)
    return (mixed / jnp.where(first, totals[0], totals[1])).astype(jnp.bfloat16)


def kernel(
    sizes,
    counts_ref, nb_ref, ns_ref, tok_hbm, wbq_hbm, wbo_hbm, wsq_hbm, wso_hbm,
    out_hbm,
    tok, wbq, wbo, wsq, wso, resid, qkv, heads, perm, perm_back, band_bias, row_bias,
    col_send, col_recv, col_out, col_ret, row_send, row_recv, row_out, row_ret, outv,
    load_sem, out_sem, cfs, cfr, crs, crr, rfs, rfr, rrs, rrr,
):
    nband, nrow, ncol, prows, pcols, slots, groups = sizes
    many = nband * nrow
    width = tok.shape[-1]
    n = prows * slots
    share = slots // many
    lines = prows // ncol
    band, row, col = (lax.axis_index(a) for a in ("band", "row", "col"))
    me = band * nrow + row

    def along(d):
        peer = lax.rem(me + d, many)
        return peer, (lax.div(peer, nrow), lax.rem(peer, nrow), col)

    def across(d):
        peer = lax.rem(col + d, ncol)
        return peer, (band, row, peer)

    barrier = pltpu.get_barrier_semaphore()
    for d in range(1, many):
        pl.semaphore_signal(barrier, inc=1, device_id=along(d)[1], device_id_type=MESH)
    for d in range(1, ncol):
        pl.semaphore_signal(barrier, inc=1, device_id=across(d)[1], device_id_type=MESH)

    loads = [pltpu.make_async_copy(tok_hbm.at[:, c], tok.at[c], load_sem.at[c]) for c in range(pcols)]
    pairs = ((wbq_hbm, wbq), (wbo_hbm, wbo), (wsq_hbm, wsq), (wso_hbm, wso))
    weights = [pltpu.make_async_copy(a, b, load_sem.at[pcols + i]) for i, (a, b) in enumerate(pairs)]
    loads[0].start()
    weights[0].start()
    for copy in loads[1:] + weights[1:]:
        copy.start()

    at = lax.broadcasted_iota(jnp.int32, (n, n), 0)
    to = lax.broadcasted_iota(jnp.int32, (n, n), 1)
    perm[...] = jnp.where(
        lax.rem(at, prows) * slots + lax.div(at, prows) == to, 1.0, 0.0
    ).astype(jnp.bfloat16)
    perm_back[...] = jnp.where(
        lax.rem(to, prows) * slots + lax.div(to, prows) == at, 1.0, 0.0
    ).astype(jnp.bfloat16)
    nblock = band_bias.shape[0]
    at = lax.broadcasted_iota(jnp.int32, (nblock, nblock), 0)
    to = lax.broadcasted_iota(jnp.int32, (nblock, nblock), 1)
    slot = lax.rem(to, slots)
    cap = slots // groups
    group = lax.div(slot, cap)
    limit = jnp.zeros_like(slot)
    for g in range(groups):
        limit = jnp.where(group == g, counts_ref[g], limit)
    keep = jnp.logical_and(
        lax.div(at, slots) == lax.div(to, slots), lax.rem(slot, cap) < limit
    )
    band_bias[...] = jnp.where(keep, 0.0, -1e30)
    rblock = row_bias.shape[0]
    unit = rblock // (ncol * pcols)
    at = lax.broadcasted_iota(jnp.int32, (rblock, rblock), 0)
    to = lax.broadcasted_iota(jnp.int32, (rblock, rblock), 1)
    row_bias[...] = jnp.where(lax.rem(at, unit) == lax.rem(to, unit), 0.0, -1e30)

    gain_band = nb_ref[...].astype(jnp.float32)
    gain_space = ns_ref[...].astype(jnp.float32)
    bw = HB * HD
    rw, cw = HR * HD, HC * HD
    sw = rw + cw
    col_fwd, row_fwd = [], []
    for c in range(pcols):
        loads[c].wait()
        x = tok[c].reshape(n, width).astype(jnp.float32)
        normed = rms_norm(x, gain_band)
        if c == 0:
            weights[0].wait()
        qkv[...] = dot(normed, wbq[...]).astype(jnp.bfloat16)
        for b in range(n // nblock):
            rows = slice(b * nblock, (b + 1) * nblock)
            for p in range(bw // PAIR):
                q, k, v = (
                    qkv[rows, t * bw + p * PAIR : t * bw + (p + 1) * PAIR] for t in range(3)
                )
                heads[rows, p * PAIR : (p + 1) * PAIR] = attend(q, k, v, band_bias[...])
        if c == 0:
            weights[1].wait()
        x = tok[c].reshape(n, width).astype(jnp.float32) + dot(heads[...], wbo[...])
        resid[c] = x
        normed = rms_norm(x, gain_space)
        if c == 0:
            weights[2].wait()
        for t in range(3):
            part = dot(normed, wsq[:, t * sw + rw : (t + 1) * sw]).astype(jnp.bfloat16)
            part = dot(perm[...], part).astype(jnp.bfloat16)
            col_send[c, :, :, t * cw : (t + 1) * cw] = part.reshape(many, share * prows, cw)
        if c == 0:
            pl.semaphore_wait(barrier, many - 1 + ncol - 1)
        fwd = []
        for d in range(1, many):
            peer, device = along(d)
            copy = pltpu.make_async_remote_copy(
                src_ref=col_send.at[c, peer],
                dst_ref=col_recv.at[c, me],
                send_sem=cfs.at[c, d],
                recv_sem=cfr.at[c, d],
                device_id=device,
                device_id_type=MESH,
            )
            copy.start()
            fwd.append(copy)
        col_fwd.append(fwd)
        for t in range(3):
            part = dot(normed, wsq[:, t * sw : t * sw + rw]).astype(jnp.bfloat16)
            row_send[c, :, :, t * rw : (t + 1) * rw] = part.reshape(ncol, lines * slots, rw)
        fwd = []
        for d in range(1, ncol):
            peer, device = across(d)
            copy = pltpu.make_async_remote_copy(
                src_ref=row_send.at[c, peer],
                dst_ref=row_recv.at[col * pcols + c],
                send_sem=rfs.at[c, d],
                recv_sem=rfr.at[c, d],
                device_id=device,
                device_id_type=MESH,
            )
            copy.start()
            fwd.append(copy)
        row_fwd.append(fwd)
        col_recv[c, me] = col_send[c, me]
        row_recv[col * pcols + c] = row_send[c, col]

    col_bwd, row_bwd = [], []

    def do_col(c):
        for copy in col_fwd[c]:
            copy.wait_recv()
        for s in range(share):
            rows = slice(s * prows, (s + 1) * prows)
            for p in range(cw // PAIR):
                q, k, v = (
                    col_recv[c, :, rows, t * cw + p * PAIR : t * cw + (p + 1) * PAIR].reshape(
                        many * prows, PAIR
                    )
                    for t in range(3)
                )
                col_out[c, :, rows, p * PAIR : (p + 1) * PAIR] = attend(q, k, v, None).reshape(
                    many, prows, PAIR
                )
        back = []
        for d in range(1, many):
            peer, device = along(d)
            copy = pltpu.make_async_remote_copy(
                src_ref=col_out.at[c, peer],
                dst_ref=col_ret.at[c, me],
                send_sem=crs.at[c, d],
                recv_sem=crr.at[c, d],
                device_id=device,
                device_id_type=MESH,
            )
            copy.start()
            back.append(copy)
        col_bwd.append(back)
        col_ret[c, me] = col_out[c, me]

    def do_row():
        for fwd in row_fwd:
            for copy in fwd:
                copy.wait_recv()
        for b in range(lines * slots // unit):
            rows = slice(b * unit, (b + 1) * unit)
            for p in range(rw // PAIR):
                q, k, v = (
                    row_recv[:, rows, t * rw + p * PAIR : t * rw + (p + 1) * PAIR].reshape(
                        rblock, PAIR
                    )
                    for t in range(3)
                )
                row_out[:, rows, p * PAIR : (p + 1) * PAIR] = attend(
                    q, k, v, row_bias[...]
                ).reshape(ncol * pcols, unit, PAIR)
        for d in range(1, ncol):
            peer, device = across(d)
            copy = pltpu.make_async_remote_copy(
                src_ref=row_out.at[pl.ds(peer * pcols, pcols)],
                dst_ref=row_ret.at[col],
                send_sem=rrs.at[d],
                recv_sem=rrr.at[d],
                device_id=device,
                device_id_type=MESH,
            )
            copy.start()
            row_bwd.append(copy)
        row_ret[col] = row_out[pl.ds(col * pcols, pcols)]

    do_col(0)
    do_row()
    for c in range(1, pcols):
        do_col(c)

    weights[3].wait()
    for copy in row_bwd:
        copy.wait_recv()
    stores = []
    for c in range(pcols):
        acc = resid[c] + dot(row_ret[:, c].reshape(n, rw), wso[:rw, :])
        for copy in col_bwd[c]:
            copy.wait_recv()
        part = dot(perm_back[...], col_ret[c].reshape(n, cw)).astype(jnp.bfloat16)
        acc = acc + dot(part, wso[rw:, :])
        outv[c] = acc.astype(jnp.bfloat16).reshape(prows, slots, width)
        store = pltpu.make_async_copy(outv.at[c], out_hbm.at[:, c], out_sem.at[c])
        store.start()
        stores.append(store)
    for copies in col_fwd + row_fwd + col_bwd + [row_bwd]:
        for copy in copies:
            copy.wait_send()
    for store in stores:
        store.wait()


def local(mesh_sizes, tokens, counts, norm_band, w_band_qkv, w_band_out, norm_space, w_space_qkv, w_space_out):
    nband, nrow, ncol = mesh_sizes
    prows, pcols, slots, width = tokens.shape
    many = nband * nrow
    n = prows * slots
    share, lines = slots // many, prows // ncol
    cols = ncol * pcols
    bands = max(1, 128 // slots) * slots
    while n % bands:
        bands -= slots
    unit = max(1, min(lines, 128 // (cols * slots)))
    while lines % unit:
        unit -= 1
    rblock = cols * unit * slots
    rw, cw = HR * HD, HC * HD
    bf16, f32 = jnp.bfloat16, jnp.float32
    vmem = pltpu.VMEM
    dma = pltpu.SemaphoreType.DMA
    sizes = (nband, nrow, ncol, prows, pcols, slots, counts.shape[0])
    anywhere = pl.BlockSpec(memory_space=pl.ANY)
    whole = pl.BlockSpec(memory_space=pltpu.VMEM)
    return pl.pallas_call(
        functools.partial(kernel, sizes),
        out_shape=jax.ShapeDtypeStruct(tokens.shape, bf16),
        in_specs=[pl.BlockSpec(memory_space=pltpu.SMEM), whole, whole] + [anywhere] * 5,
        out_specs=anywhere,
        scratch_shapes=[
            vmem((pcols, prows, slots, width), bf16),
            vmem(w_band_qkv.shape, bf16),
            vmem(w_band_out.shape, bf16),
            vmem(w_space_qkv.shape, bf16),
            vmem(w_space_out.shape, bf16),
            vmem((pcols, n, width), f32),
            vmem((n, 3 * HB * HD), bf16),
            vmem((n, HB * HD), bf16),
            vmem((n, n), bf16),
            vmem((n, n), bf16),
            vmem((bands, bands), f32),
            vmem((rblock, rblock), f32),
            vmem((pcols, many, share * prows, 3 * cw), bf16),
            vmem((pcols, many, share * prows, 3 * cw), bf16),
            vmem((pcols, many, share * prows, cw), bf16),
            vmem((pcols, many, share * prows, cw), bf16),
            vmem((pcols, ncol, lines * slots, 3 * rw), bf16),
            vmem((cols, lines * slots, 3 * rw), bf16),
            vmem((cols, lines * slots, rw), bf16),
            vmem((ncol, pcols, lines * slots, rw), bf16),
            vmem((pcols, prows, slots, width), bf16),
            dma((pcols + 4,)),
            dma((pcols,)),
            dma((pcols, many)),
            dma((pcols, many)),
            dma((pcols, many)),
            dma((pcols, many)),
            dma((pcols, ncol)),
            dma((pcols, ncol)),
            dma((ncol,)),
            dma((ncol,)),
        ],
        compiler_params=pltpu.CompilerParams(
            collective_id=0, has_side_effects=True, vmem_limit_bytes=48 * 1024 * 1024
        ),
        cost_estimate=pl.CostEstimate(
            flops=12 * prows * pcols * slots * width * width // 2,
            bytes_accessed=12 * 1024 * 1024,
            transcendentals=4 * 1024 * 1024,
        ),
    )(
        counts,
        norm_band.reshape(1, -1),
        norm_space.reshape(1, -1),
        tokens,
        w_band_qkv,
        w_band_out,
        w_space_qkv,
        w_space_out,
    )


def solution(mesh):
    sizes = tuple(mesh.shape[a] for a in ("band", "row", "col"))
    placed = (P(("band", "row"), "col", None, None), P(), P(), P(), P(), P(), P(), P())
    return jax.shard_map(
        functools.partial(local, sizes),
        mesh=mesh,
        in_specs=placed,
        out_specs=P(("band", "row"), "col", None, None),
        check_vma=False,
    )
```

time: 159 us -> 43.2 us (0.27)
  waiting for transfers between devices: 49.4 us -> 0 us
  local copies, waits for them, and re-layouts: 45 us -> 6.67 us
  Pallas kernels: 0 us -> 36.2 us
  matrix products: 23.4 us -> 0 us
  blocking collectives: 14.9 us -> 0 us
  between operations: 13.7 us -> 0.01 us
  other arithmetic: 8.25 us -> 0 us
  starting transfers between devices: 3.67 us -> 0 us
    all_gather x1 -> x0, waiting for transfers between devices: 46.1 us -> none  [local(): lax.all_gather(col_part[:, :, :, 1:], ('band', 'row'), axis=0, tiled=True)]
    pallas_call x0 -> x1, Pallas kernels: none -> 36.2 us  [local(): pl.pallas_call(functools.partial(kernel, sizes), out_shape=jax.ShapeDtype...]
    slice x11 -> x0, local copies, waits for them, and re-layouts: 27.6 us -> none  [the longest x2 13.5 us: local(): keys = piece[:, :, :, 0].reshape(many, pcols, slots, HC, HD)]
    dot_general x10 -> x0, matrix products: 23.4 us -> none  [the longest x1 3.82 us: local(): jnp.dot(heads.reshape(-1, (HR + HC) * HD), w_space_out, preferred_element...]
    all_to_all x1 -> x0, blocking collectives: 14.9 us -> none  [local(): lax.all_to_all(row_part, 'col', split_axis=0, concat_axis=1, tiled=True)]
    reshape x5 -> x2, local copies, waits for them, and re-layouts: 11.6 us -> 1.37 us  [the longest x1 0.69 us: local(): norm_band.reshape(1, -1)]
    reduce_sum x5 -> x0, other arithmetic: 5 us -> none  [the longest x1 1.51 us: rms_norm(): scale = lax.rsqrt(jnp.mean(wide * wide, axis=-1, keepdims=True) + EPS)]
    all_to_all x1 -> x0, starting transfers between devices: 3.67 us -> none  [local(): lax.all_to_all(line_mixed, 'col', split_axis=1, concat_axis=0, tiled=True)]
  transfers between devices with their start and end apart: 2 -> 0, of which waited for: 2 -> 0; matrix products, arithmetic and copies ran while one was open for 6% -> 0% of each run, Pallas kernels for 0% -> 0%
where the time goes in v1:
time: 43.2 us; the launch traced here: 42.9 us
  Pallas kernels  36.2 us (84%)
  local copies, waits for them, and re-layouts  6.67 us (15%)
    pallas_call x1, Pallas kernels, local(): pl.pallas_call(functools.partial(kernel, sizes), out_shape=jax.ShapeDtype...  36.2 us
    unnamed x9, local copies, waits for them, and re-layouts  5.3 us

profile of v1, /device:TPU:0, one launch (start us, length us, event | category | flops | bytes accessed | tf_op | source)
XLA Modules:
  0.0 42.9 jit_solution(5662415413695946378)
XLA Ops:
  0.0 0.7 %reshape.6.nb_ref = bf16[1,1024]{1,0:T(2,128)(2,1)S(1)} reshape(bf16[1024]{0:T(1024)(128)(2,1)} %param.10) | data formatting | bytes 4096 | tf_op jit(solution)/shard_map/reshape | solution.py:348
  0.7 0.7 %reshape.7.ns_ref = bf16[1,1024]{1,0:T(2,128)(2,1)S(1)} reshape(bf16[1024]{0:T(1024)(128)(2,1)} %param.13) | data formatting | bytes 4096 | tf_op jit(solution)/shard_map/reshape | solution.py:349
  1.4 0.0 copy-start
  1.4 1.2 %copy-done = bf16[16,2,16,1024]{3,2,1,0:T(8,128)(2,1)S(1)} copy-done((bf16[16,2,16,1024]{3,2,1,0:T(8,128)(2,1)S(1)}, bf16[16,2,16,1024]{3,2,1,0:T(8,128)(2,1)}, u32[]{:S(2)}) %copy-start) | copy-done | bytes 1048600
  2.6 0.0 copy-start.1
  2.6 1.2 %copy-done.1 = bf16[512,1024]{1,0:T(8,128)(2,1)S(1)} copy-done((bf16[512,1024]{1,0:T(8,128)(2,1)S(1)}, bf16[512,1024]{1,0:T(8,128)(2,1)}, u32[]{:S(2)}) %copy-start.1) | copy-done | bytes 1048600
  3.8 0.0 copy-start.2
  3.8 1.2 %copy-done.2 = bf16[512,1024]{1,0:T(8,128)(2,1)S(1)} copy-done((bf16[512,1024]{1,0:T(8,128)(2,1)S(1)}, bf16[512,1024]{1,0:T(8,128)(2,1)}, u32[]{:S(2)}) %copy-start.2) | copy-done | bytes 1048600
  5.0 0.0 copy-start.3
  5.0 0.7 %copy-done.3 = s32[4]{0:T(128)S(1)} copy-done((s32[4]{0:T(128)S(1)}, s32[4]{0:T(128)}, u32[]{:S(2)}) %copy-start.3) | copy-done | bytes 40
  5.7 36.2 %shard_map.82 = bf16[16,2,16,1024]{3,2,1,0:T(8,128)(2,1)S(1)} custom-call(s32[4]{0:T(128)S(1)} %copy-done.3, bf16[1,1024]{1,0:T(2,128)(2,1)S(1)} %reshape.6.nb_ref, bf16[1,1024]{1,0:T(2,128)(2,1)S(1)} %reshape.7.ns_ref, bf16[16,2,16,1024]{3,2,1,0:T(8,128)(2,1)S(1)} %copy-done, bf16[1024,1536]{1,0:T(8,128)(2,1)} %wbq_hbm.1, bf16[512,1024]{1,0:T(8,128)(2,1)S(1)} %copy-done.1, ...), custom_call_target="tpu_custom_call" | custom-call | flops 3221225472 | bytes 12582912 | tf_op jit(solution)/shard_map/pallas_call | solution.py:300
  41.9 1.0 %copy.10 = bf16[16,2,16,1024]{3,2,1,0:T(8,128)(2,1)} copy(bf16[16,2,16,1024]{3,2,1,0:T(8,128)(2,1)S(1)} %shard_map.82) | data formatting | bytes 2097152
Async XLA Ops:
  1.4 1.2 %copy-start = (bf16[16,2,16,1024]{3,2,1,0:T(8,128)(2,1)S(1)}, bf16[16,2,16,1024]{3,2,1,0:T(8,128)(2,1)}, u32[]{:S(2)}) copy-start(bf16[16,2,16,1024]{3,2,1,0:T(8,128)(2,1)} %tok_hbm.1) | copy-start | bytes 3145732
  2.6 1.2 %copy-start.1 = (bf16[512,1024]{1,0:T(8,128)(2,1)S(1)}, bf16[512,1024]{1,0:T(8,128)(2,1)}, u32[]{:S(2)}) copy-start(bf16[512,1024]{1,0:T(8,128)(2,1)} %wbo_hbm.1) | copy-start | bytes 3145732
  3.8 1.2 %copy-start.2 = (bf16[512,1024]{1,0:T(8,128)(2,1)S(1)}, bf16[512,1024]{1,0:T(8,128)(2,1)}, u32[]{:S(2)}) copy-start(bf16[512,1024]{1,0:T(8,128)(2,1)} %wso_hbm.1) | copy-start | bytes 3145732
  5.0 0.7 %copy-start.3 = (s32[4]{0:T(128)S(1)}, s32[4]{0:T(128)}, u32[]{:S(2)}) copy-start(s32[4]{0:T(128)} %counts_ref.1) | copy-start | bytes 52

commit v2 on v1

--- a/solution.py
+++ b/solution.py
@@ -17,6 +17,7 @@
 LOG2E = 1.4426950408889634
 MESH = pl.DeviceIdType.MESH
 PAIR = 2 * HD
+LIMIT = 63 * 1024 * 1024
 
 
 def rms_norm(wide, gain):
@@ -56,11 +57,11 @@
 
 def kernel(
     sizes,
-    counts_ref, nb_ref, ns_ref, tok_hbm, wbq_hbm, wbo_hbm, wsq_hbm, wso_hbm,
+    counts_hbm, nb_hbm, ns_hbm, tok_hbm, wbq_hbm, wbo_hbm, wsq_hbm, wso_hbm,
     out_hbm,
     tok, wbq, wbo, wsq, wso, resid, qkv, heads, perm, perm_back, band_bias, row_bias,
     col_send, col_recv, col_out, col_ret, row_send, row_recv, row_out, row_ret, outv,
-    load_sem, out_sem, cfs, cfr, crs, crr, rfs, rfr, rrs, rrr,
+    counts_ref, nb_ref, ns_ref, load_sem, out_sem, cfs, cfr, crs, crr, rfs, rfr, rrs, rrr,
 ):
     nband, nrow, ncol, prows, pcols, slots, groups = sizes
     many = nband * nrow
@@ -88,7 +89,11 @@
     loads = [pltpu.make_async_copy(tok_hbm.at[:, c], tok.at[c], load_sem.at[c]) for c in range(pcols)]
     pairs = ((wbq_hbm, wbq), (wbo_hbm, wbo), (wsq_hbm, wsq), (wso_hbm, wso))
     weights = [pltpu.make_async_copy(a, b, load_sem.at[pcols + i]) for i, (a, b) in enumerate(pairs)]
+    small = ((counts_hbm, counts_ref), (nb_hbm, nb_ref), (ns_hbm, ns_ref))
+    small = [pltpu.make_async_copy(a, b, load_sem.at[pcols + 4 + i]) for i, (a, b) in enumerate(small)]
     loads[0].start()
+    for copy in small:
+        copy.start()
     weights[0].start()
     for copy in loads[1:] + weights[1:]:
         copy.start()
@@ -101,6 +106,8 @@
     perm_back[...] = jnp.where(
         lax.rem(to, prows) * slots + lax.div(to, prows) == at, 1.0, 0.0
     ).astype(jnp.bfloat16)
+    for copy in small:
+        copy.wait()
     nblock = band_bias.shape[0]
     at = lax.broadcasted_iota(jnp.int32, (nblock, nblock), 0)
     to = lax.broadcasted_iota(jnp.int32, (nblock, nblock), 1)
@@ -120,8 +127,8 @@
     to = lax.broadcasted_iota(jnp.int32, (rblock, rblock), 1)
     row_bias[...] = jnp.where(lax.rem(at, unit) == lax.rem(to, unit), 0.0, -1e30)
 
-    gain_band = nb_ref[...].astype(jnp.float32)
-    gain_space = ns_ref[...].astype(jnp.float32)
+    gain_band = nb_ref[...].astype(jnp.float32).reshape(1, width)
+    gain_space = ns_ref[...].astype(jnp.float32).reshape(1, width)
     bw = HB * HD
     rw, cw = HR * HD, HC * HD
     sw = rw + cw
@@ -295,12 +302,11 @@
     vmem = pltpu.VMEM
     dma = pltpu.SemaphoreType.DMA
     sizes = (nband, nrow, ncol, prows, pcols, slots, counts.shape[0])
-    anywhere = pl.BlockSpec(memory_space=pl.ANY)
-    whole = pl.BlockSpec(memory_space=pltpu.VMEM)
+    anywhere = pl.BlockSpec(memory_space=pltpu.HBM)
     return pl.pallas_call(
         functools.partial(kernel, sizes),
         out_shape=jax.ShapeDtypeStruct(tokens.shape, bf16),
-        in_specs=[pl.BlockSpec(memory_space=pltpu.SMEM), whole, whole] + [anywhere] * 5,
+        in_specs=[anywhere] * 8,
         out_specs=anywhere,
         scratch_shapes=[
             vmem((pcols, prows, slots, width), bf16),
@@ -324,7 +330,10 @@
             vmem((cols, lines * slots, rw), bf16),
             vmem((ncol, pcols, lines * slots, rw), bf16),
             vmem((pcols, prows, slots, width), bf16),
-            dma((pcols + 4,)),
+            pltpu.SMEM(counts.shape, jnp.int32),
+            vmem(norm_band.shape, bf16),
+            vmem(norm_space.shape, bf16),
+            dma((pcols + 7,)),
             dma((pcols,)),
             dma((pcols, many)),
             dma((pcols, many)),
@@ -336,7 +345,7 @@
             dma((ncol,)),
         ],
         compiler_params=pltpu.CompilerParams(
-            collective_id=0, has_side_effects=True, vmem_limit_bytes=48 * 1024 * 1024
+            collective_id=0, has_side_effects=True, vmem_limit_bytes=LIMIT
         ),
         cost_estimate=pl.CostEstimate(
             flops=12 * prows * pcols * slots * width * width // 2,
@@ -345,8 +354,8 @@
         ),
     )(
         counts,
-        norm_band.reshape(1, -1),
-        norm_space.reshape(1, -1),
+        norm_band,
+        norm_space,
         tokens,
         w_band_qkv,
         w_band_out,

time: 43.2 us -> 38.9 us (0.900)
  local copies, waits for them, and re-layouts: 6.67 us -> 2.31 us
    unnamed x9 -> x1, local copies, waits for them, and re-layouts: 5.3 us -> 2.31 us
    reshape x2 -> x0, local copies, waits for them, and re-layouts: 1.37 us -> none  [the longest x1 0.69 us: local(): norm_band.reshape(1, -1)]
where the time goes in v2:
time: 38.9 us; the launch traced here: 38.7 us
  Pallas kernels  36.4 us (94%)
  local copies, waits for them, and re-layouts  2.31 us (6%)
    pallas_call x1, Pallas kernels, local(): pl.pallas_call(functools.partial(kernel, sizes), out_shape=jax.ShapeDtype...  36.4 us
    unnamed x1, local copies, waits for them, and re-layouts  2.31 us

profile of v2, /device:TPU:0, one launch (start us, length us, event | category | flops | bytes accessed | tf_op | source)
XLA Modules:
  0.0 38.7 jit_solution(14598669649896269499)
XLA Ops:
  0.0 36.4 %shard_map.82 = bf16[16,2,16,1024]{3,2,1,0:T(8,128)(2,1)} custom-call(s32[4]{0:T(128)} %counts_hbm.1, bf16[1024]{0:T(1024)(128)(2,1)} %nb_hbm.1, bf16[1024]{0:T(1024)(128)(2,1)} %ns_hbm.1, bf16[16,2,16,1024]{3,2,1,0:T(8,128)(2,1)} %tok_hbm.1, bf16[1024,1536]{1,0:T(8,128)(2,1)} %wbq_hbm.1, bf16[512,1024]{1,0:T(8,128)(2,1)} %wbo_hbm.1, ...), custom_call_target="tpu_custom_call" | custom-call | flops 3221225472 | bytes 12582912 | tf_op jit(solution)/shard_map/pallas_call | solution.py:306
  36.4 2.3 %copy.10 = bf16[16,2,16,1024]{3,2,1,0:T(8,128)(2,1)} copy(bf16[16,2,16,1024]{3,2,1,0:T(8,128)(2,1)} %shard_map.82) | data formatting | bytes 2097152
